TPU v7x, 32 devices: a whole 2x2x4 slice. The times are simulated.
32 devices in a mesh: seq: 8 (over z, x), head: 4 (over y, core).
Axes of the slice: x: 2, y: 2, z: 4, core: 2. Of those that a mesh axis runs over, the one named last changes fastest.
Arguments:
- queries: bfloat16 [4096, 4096], P('seq', 'head'), may hold values from -6 to 6
- key_rows: bfloat16 [4096, 4096], P('seq', 'head'), may hold values from -6 to 6
- value_rows: bfloat16 [4096, 4096], P('seq', 'head'), may hold values from -18 to 18
- out_grad: bfloat16 [4096, 4096], P('seq', 'head'), may hold values from -6 to 6
- log_decay: float32 [32, 4096], P('head', 'seq'), may hold values from -0.6 to 0
Outputs:
- query_gradient: bfloat16 [4096, 4096], P('seq', 'head')
- key_grad: bfloat16 [4096, 4096], P('seq', 'head')
- value_grad: bfloat16 [4096, 4096], P('seq', 'head')
All inputs are finite; a program needn't handle non-finite values.
Results may differ from a plain program's by a relative error of at most 0.006.
Values sent between devices are 32-bit elements; how exact they have to be, the bound alone decides.
A program may use at most 64 MiB of HBM per device.

v0:
```python
import jax
import jax.numpy as jnp
from jax import lax
from jax.sharding import PartitionSpec as P

HEAD_COUNT = 32
DH = 128
BLOCK = 128


epsilon = 1e-06
highest = lax.Precision.HIGHEST


def shards(queries, key_rows, value_rows, out_grad, log_decay):
    tok_rows, row_width = queries.shape
    heads_dev = log_decay.shape[0]
    head_size = row_width // heads_dev
    blocks = tok_rows // BLOCK
    total_width = HEAD_COUNT * DH
    block_shape = (blocks, BLOCK, heads_dev, head_size)
    query_block_rows = queries.reshape(block_shape)
    key_blocks = key_rows.reshape(block_shape)
    value_block_rows = value_rows.reshape(block_shape)
    grad_blocks = out_grad.reshape(block_shape)
    decay_blocks = jnp.transpose(log_decay.reshape(heads_dev, blocks, BLOCK), (1, 2, 0))
    inside_block_mask = jnp.cumsum(decay_blocks, axis=1)
    totals = inside_block_mask[:, -1, :]
    before = jnp.cumsum(totals, axis=0) - totals
    shard_total = jnp.sum(totals, axis=0)
    token_positions = jnp.arange(BLOCK)
    causal = (token_positions[:, None] >= token_positions[None, :]).astype(jnp.float32)
    within_heads = jnp.transpose(inside_block_mask, (0, 2, 1))
    exponent = within_heads[:, :, :, None] - within_heads[:, :, None, :]
    decay_mask = jnp.exp(jnp.minimum(exponent, 0.0)) * causal
    scores = jnp.einsum(
        "nihd,njhd->nhij", query_block_rows, key_blocks, preferred_element_type=jnp.float32
    )
    attention_weights = (scores * decay_mask).astype(jnp.bfloat16)
    intra_out = jnp.einsum(
        "nhij,njhd->nihd", attention_weights, value_block_rows, preferred_element_type=jnp.float32
    )
    to_end = jnp.exp(totals[:, None, :] - inside_block_mask)
    keys_scaled = (to_end[..., None] * key_blocks).astype(jnp.bfloat16)
    block_terms = jnp.einsum(
        "njhd,njhe->nhde", keys_scaled, value_block_rows, preferred_element_type=jnp.float32
    )
    block_ids = jnp.arange(blocks)
    earlier_blocks = (block_ids[:, None] > block_ids[None, :]).astype(jnp.float32)
    forward_exp = before[:, None, :] - before[None, :, :] - totals[None, :, :]
    forward_mix = jnp.exp(jnp.minimum(forward_exp, 0.0)) * earlier_blocks[:, :, None]
    local_states = jnp.einsum("nmh,mhde->nhde", forward_mix, block_terms, precision=highest)
    shard_state = jnp.einsum(
        "mh,mhde->hde",
        jnp.exp(shard_total[None, :] - before - totals),
        block_terms,
        precision=highest,
    )
    all_totals, all_states = (
        lax.all_gather(shard_total[None], "seq", axis=0, tiled=True),
        lax.all_gather(shard_state[None], "seq", axis=0, tiled=True),
    )
    seq_ranks = lax.axis_size("seq")
    my_rank = lax.axis_index("seq")
    starts = jnp.cumsum(all_totals, axis=0) - all_totals
    my_start = lax.dynamic_index_in_dim(starts, my_rank, 0, keepdims=False)
    rank_ids = jnp.arange(seq_ranks)
    reach_log = my_start[None, :] - starts - all_totals
    mixing = jnp.exp(jnp.minimum(reach_log, 0.0)) * (rank_ids < my_rank)[:, None].astype(
        jnp.float32
    )
    incoming = jnp.einsum("rh,rhde->hde", mixing, all_states, precision=highest)
    states = local_states + jnp.exp(before)[:, :, None, None] * incoming[None]
    backward_state = states.astype(jnp.bfloat16)
    inter_out = jnp.einsum(
        "nihd,nhde->nihe", query_block_rows, backward_state, preferred_element_type=jnp.float32
    )
    attention_output = intra_out + jnp.exp(inside_block_mask)[..., None] * inter_out
    square = jnp.sum(attention_output * attention_output, axis=(2, 3))
    square_total = lax.psum(square, "head")
    inv_rms = lax.rsqrt(square_total / total_width + epsilon)
    normed = attention_output * inv_rms[:, :, None, None]
    cross_local = jnp.sum(grad_blocks.astype(jnp.float32) * normed, axis=(2, 3))
    cross_total = lax.psum(cross_local, "head")
    mean_cross = cross_total / total_width
    attention_gradient = (
        inv_rms[:, :, None, None]
        * (grad_blocks.astype(jnp.float32) - normed * mean_cross[:, :, None, None])
    ).astype(jnp.bfloat16)
    score_gradient = jnp.einsum(
        "nihe,njhe->nhij", attention_gradient, value_block_rows, preferred_element_type=jnp.float32
    )
    grad_probs = (score_gradient * decay_mask).astype(jnp.bfloat16)
    query_gradient = jnp.einsum(
        "nhij,njhd->nihd", grad_probs, key_blocks, preferred_element_type=jnp.float32
    )
    query_gradient = query_gradient + jnp.exp(inside_block_mask)[..., None] * jnp.einsum(
        "nihe,nhde->nihd", attention_gradient, backward_state, preferred_element_type=jnp.float32
    )
    key_intra = jnp.einsum(
        "nhij,nihd->njhd", grad_probs, query_block_rows, preferred_element_type=jnp.float32
    )
    value_within_block = jnp.einsum(
        "nhij,nihe->njhe", attention_weights, attention_gradient, preferred_element_type=jnp.float32
    )
    scaled_query_rows = (jnp.exp(inside_block_mask)[..., None] * query_block_rows).astype(
        jnp.bfloat16
    )
    backward_terms = jnp.einsum(
        "nihd,nihe->nhde", scaled_query_rows, attention_gradient, preferred_element_type=jnp.float32
    )
    later_blocks = (block_ids[:, None] < block_ids[None, :]).astype(jnp.float32)
    backward_exp = before[None, :, :] - before[:, None, :] - totals[:, None, :]
    backward_mix = jnp.exp(jnp.minimum(backward_exp, 0.0)) * later_blocks[:, :, None]
    local_back = jnp.einsum("nmh,mhde->nhde", backward_mix, backward_terms, precision=highest)
    shard_back = jnp.einsum("mh,mhde->hde", jnp.exp(before), backward_terms, precision=highest)
    shard_piece = lax.all_gather(shard_back[None], "seq", axis=0, tiled=True)
    piece_rows = shard_piece.shape[0]
    piece_ranks = jnp.arange(piece_rows)
    reach_log = starts - my_start[None, :] - shard_total[None, :]
    mixing = jnp.exp(jnp.minimum(reach_log, 0.0)) * (piece_ranks > my_rank)[:, None].astype(
        jnp.float32
    )
    later_state = jnp.einsum("rh,rhde->hde", mixing, shard_piece, precision=highest)
    back_states = (
        local_back
        + jnp.exp(shard_total[None, :] - before - totals)[:, :, None, None] * later_state[None]
    )
    back_b = back_states.astype(jnp.bfloat16)
    key_grad = key_intra + to_end[..., None] * jnp.einsum(
        "njhe,nhde->njhd", value_block_rows, back_b, preferred_element_type=jnp.float32
    )
    value_grad = value_within_block + to_end[..., None] * jnp.einsum(
        "njhd,nhde->njhe", key_blocks, back_b, preferred_element_type=jnp.float32
    )
    return (
        query_gradient.reshape(tok_rows, row_width).astype(jnp.bfloat16),
        key_grad.reshape(tok_rows, row_width).astype(jnp.bfloat16),
        value_grad.reshape(tok_rows, row_width).astype(jnp.bfloat16),
    )


def solution(mesh):
    return jax.shard_map(
        shards,
        mesh=mesh,
        in_specs=(
            P("seq", "head"),
            P("seq", "head"),
            P("seq", "head"),
            P("seq", "head"),
            P("head", "seq"),
        ),
        out_specs=(P("seq", "head"), P("seq", "head"), P("seq", "head")),
        check_vma=False,
    )
```

profile of v0, /device:TPU:0, one launch (start us, length us, event | category | flops | bytes accessed | tf_op | source)
XLA Modules:
  0.0 232.3 jit_solution(4838523320197504257)
XLA Ops:
  7.2 0.9 copy.88
  8.1 0.3 reduce_window_sum.35
  8.8 0.3 copy.152
  9.1 1.0 copy-done.21
  10.0 0.3 copy.153
  10.3 1.8 fusion.25
  12.2 5.0 %fusion.17 = f32[8,1,128,128]{3,1,2,0:T(1,128)} fusion(f32[4,8,1,1]{0,2,3,1:T(1,128)S(1)} %copy.132, f32[4,8,128,128]{3,2,1,0:T(8,128)S(1)} %fusion.25), kind=kOutput, calls=%fused_computation.32 | convolution fusion | flops 6291456 | bytes 2621568 | tf_op jit(solution)/shard_map/mh,mhde->hde/dot_general | solution.py:53
  17.4 0.6 dynamic-slice
  18.6 0.2 dynamic-update-slice
  18.9 23.5 %all-reduce = f32[64]{0:T(128)S(1)} all-reduce(f32[64]{0:T(128)S(1)} %dynamic-update-slice), channel_id=2, replica_groups=mesh['seq'=8,'head'=4] {'seq'}, use_global_device_ids=true, to_apply=%add | all-reduce | flops 64 | bytes 512
  43.0 1.6 copy.151
  44.5 1.5 copy.116
  46.1 0.3 convert_bitcast_fusion
  46.4 1.8 copy.154
  48.2 1.9 copy.106
  50.2 2.7 %multiply_convert_fusion.4 = bf16[4,8,128,128]{3,2,1,0:T(8,128)(2,1)S(1)} fusion(bf16[4,128,8,128]{1,3,2,0:T(8,128)(2,1)} %copy.116, f32[128,128]{1,0:T(8,128)S(1)} %fusion.41, f32[4,8,128]{2,1,0:T(8,128)S(1)} %copy.89, bf16[4,128,8,128]{3,2,1,0:T(8,128)(2,1)} %bitcast.126), kind=kOutput, calls=%fused_computation.26 | convolution fusion | flops 136839168 | bytes 3227648 | tf_op jit(solution)/shard_map/nihd,njhd->nhij/dot_general | solution.py:36
  52.9 1.0 copy-done.15
  53.9 2.2 fusion.31
  56.2 37.4 %all-gather.6.cloned.1.call-done = f32[64,128,128]{2,1,0:T(8,128)} async-done(((f32[8,128,128]{2,1,0:T(8,128)}), f32[64,128,128]{2,1,0:T(8,128)}) %all-gather.6.cloned.1.call-update) | async-done | bytes 4194320 | tf_op jit(solution)/shard_map/all_gather | solution.py:61
  93.6 8.3 %fusion.2 = f32[8,1,128,128]{3,1,2,0:T(1,128)S(1)} fusion(f32[8,8,1,1]{0,2,3,1:T(1,128)S(1)} %copy.134, f32[8,8,128,128]{3,2,1,0:T(8,128)} %bitcast.130), kind=kOutput, calls=%fused_computation.2 | convolution fusion | flops 12582912 | bytes 4718848 | tf_op jit(solution)/shard_map/rh,rhde->hde/dot_general | solution.py:72
  102.0 4.9 %fusion.12 = bf16[4,8,128,128]{3,0,2,1:T(4,128)(2,1)S(1)} fusion(f32[4,8,128,128]{3,2,1,0:T(8,128)S(1)} %copy-done.8, f32[8,128,128]{2,1,0:T(8,128)S(1)} %bitcast.147, f32[4,8]{0,1:T(8,128)S(1)} %copy.102, f32[4,4]{1,0:T(4,128)S(1)} %fusion.64, f32[4,8]{0,1:T(8,128)S(1)} %copy.100, f32[4,8]{0,1:T(8,128)S(1)} %copy.99, f32[4,8]{0,1:T(8,128)S(1)} %copy.98), kind=kOutput, calls=%fused_computation.18 | convolution fusion | flops 26739200 | bytes 3670592 | tf_op jit(solution)/shard_map/nmh,mhde->nhde/dot_general | solution.py:52
  106.9 2.0 multiply_reduce_fusion.1
  108.9 5.6 %psum.14 = f32[4,128]{1,0:T(4,128)S(1)} all-reduce(f32[4,128]{1,0:T(4,128)S(1)} %get-tuple-element.13), channel_id=1, replica_groups=mesh['seq'=8,'head'=4] {'head'}, use_global_device_ids=true, to_apply=%region_5.6 | all-reduce | flops 512 | bytes 4096 | tf_op jit(solution)/shard_map/psum | solution.py:80
  114.5 1.8 multiply_reduce_fusion
  116.3 6.6 %psum.15 = f32[4,128]{1,0:T(4,128)S(1)} all-reduce(f32[4,128]{1,0:T(4,128)S(1)} %multiply_reduce_fusion), channel_id=1, replica_groups=mesh['seq'=8,'head'=4] {'head'}, use_global_device_ids=true, to_apply=%region_7.8 | all-reduce | flops 512 | bytes 4096 | tf_op jit(solution)/shard_map/psum | solution.py:84
  123.0 2.1 multiply_convert_fusion.2
  125.1 0.8 fusion.26
  126.0 0.1 copy-done.2
  126.1 5.0 %fusion.13 = f32[8,1,128,128]{3,1,2,0:T(1,128)} fusion(f32[4,8,1,1]{0,2,3,1:T(1,128)S(1)} %copy.143, f32[4,8,128,128]{3,2,1,0:T(8,128)S(1)} %fusion.26), kind=kOutput, calls=%fused_computation.28 | convolution fusion | flops 6291456 | bytes 2621568 | tf_op jit(solution)/shard_map/mh,mhde->hde/dot_general | solution.py:116
  131.2 2.4 %multiply_convert_fusion.1 = bf16[4,8,128,128]{3,2,1,0:T(8,128)(2,1)S(1)} fusion(bf16[4,128,8,128]{1,3,2,0:T(8,128)(2,1)} %copy-done.2, f32[128,128]{1,0:T(8,128)S(1)} %fusion.41, f32[4,8,128]{2,1,0:T(8,128)S(1)} %copy.89, bf16[4,128,8,128]{3,2,1,0:T(8,128)(2,1)S(1)} %bitcast.123), kind=kOutput, calls=%fused_computation.21 | convolution fusion | flops 136839168 | bytes 3227648 | tf_op jit(solution)/shard_map/nihe,njhe->nhij/dot_general | solution.py:90
  133.7 0.9 fusion.37
  134.6 0.7 copy-done.3
  135.3 0.3 copy-done.14
  135.6 1.5 fusion.10
  137.1 2.6 %copy.113 = bf16[4,128,8,128]{3,2,1,0:T(8,128)(2,1)} copy(bf16[4,128,8,128]{1,3,2,0:T(8,128)(2,1)} %fusion.10) | data formatting | bytes 2097152 | tf_op jit(solution)/shard_map/convert_element_type | solution.py:137
  139.7 2.6 %copy.203 = bf16[64,8,8,128]{3,1,2,0:T(8,128)(2,1)} copy(bf16[64,8,8,128]{3,2,1,0:T(8,128)(2,1)} %bitcast.132) | data formatting | bytes 2097152
  142.3 2.2 fusion.70
  144.5 2.2 fusion.69
  146.8 55.7 %all-gather.8.cloned.1.call-done = f32[64,128,128]{2,1,0:T(8,128)} async-done(((f32[8,128,128]{2,1,0:T(8,128)}), f32[64,128,128]{2,1,0:T(8,128)}) %all-gather.8.cloned.1.call-update) | async-done | bytes 4194320 | tf_op jit(solution)/shard_map/all_gather | solution.py:117
  202.5 8.4 %fusion = f32[8,1,128,128]{3,1,2,0:T(1,128)S(1)} fusion(f32[8,8,1,1]{0,2,3,1:T(1,128)S(1)} %copy.145, f32[8,8,128,128]{3,2,1,0:T(8,128)} %bitcast.131), kind=kOutput, calls=%fused_computation | convolution fusion | flops 12582912 | bytes 4718848 | tf_op jit(solution)/shard_map/rh,rhde->hde/dot_general | solution.py:124
  210.8 5.5 %fusion.8 = bf16[4,8,128,128]{3,0,2,1:T(4,128)(2,1)} fusion(f32[4,8,128,128]{3,2,1,0:T(8,128)S(1)} %copy-done.10, f32[8,128,128]{2,1,0:T(8,128)S(1)} %bitcast.146, f32[4,8]{0,1:T(8,128)S(1)} %copy.120, f32[4,4]{1,0:T(4,128)S(1)} %fusion.65, f32[4,8]{0,1:T(8,128)S(1)} %copy.100, f32[4,8]{0,1:T(8,128)S(1)} %copy.99, f32[4,8]{0,1:T(8,128)S(1)} %copy.98), kind=kOutput, calls=%fused_computation.11 | convolution fusion | flops 26739200 | bytes 3670592 | tf_op jit(solution)/shard_map/nmh,mhde->nhde/dot_general | solution.py:115
  216.3 1.7 copy.126
  218.1 2.2 fusion.5
  220.3 0.7 copy.129
  221.0 1.2 copy.201
  222.3 0.8 fusion.7
  223.1 0.7 copy.124
  223.7 1.3 copy.202
  (75 shorter events, 1.6 us)
Async XLA Ops:
  7.2 1.6 copy-start.20
  7.2 86.4 %all-gather.6.cloned.1.call-start = ((), (), s32[]{:S(2)}) async-start(), calls=%async_computation | async-start | bytes 4718592 | tf_op jit(solution)/shard_map/all_gather | solution.py:61
  8.8 1.3 copy-start.21
  9.1 3.1 %copy-start = (bf16[64,8,8,128]{3,2,1,0:T(8,128)(2,1)}, bf16[64,8,8,128]{3,2,1,0:T(8,128)(2,1)S(1)}, u32[]{:S(2)}) copy-start(bf16[64,8,8,128]{3,2,1,0:T(8,128)(2,1)S(1)} %copy.152) | copy-start | bytes 3145732
  12.1 5.0 %copy-start.7 = (f32[4,8,128,128]{3,2,1,0:T(8,128)}, f32[4,8,128,128]{3,2,1,0:T(8,128)S(1)}, u32[]{:S(2)}) copy-start(f32[4,8,128,128]{3,2,1,0:T(8,128)S(1)} %fusion.25) | copy-start | bytes 6291460
  12.2 5.2 %copy-start.22 = (u32[32]{0:T(128)S(1)}, u32[32]{0:T(128)}, u32[]{:S(2)}) copy-start(u32[32]{0:T(128)} %constant.34) | copy-start | bytes 388
  17.2 185.3 %all-gather.8.cloned.1.call-start = ((), (), s32[]{:S(2)}) async-start(), calls=%async_computation.1 | async-start | bytes 4718592 | tf_op jit(solution)/shard_map/all_gather | solution.py:117
  43.0 3.2 %copy-start.19 = (bf16[512,1024]{1,0:T(8,128)(2,1)S(1)}, bf16[512,1024]{1,0:T(8,128)(2,1)}, u32[]{:S(2)}) copy-start(bf16[512,1024]{1,0:T(8,128)(2,1)} %param.8) | copy-start | bytes 3145732
  52.9 1.1 copy-start.15
  93.6 8.4 %copy-start.8 = (f32[4,8,128,128]{3,2,1,0:T(8,128)S(1)}, f32[4,8,128,128]{3,2,1,0:T(8,128)}, u32[]{:S(2)}) copy-start(f32[4,8,128,128]{3,2,1,0:T(8,128)} %copy-done.7) | copy-start | bytes 6291460
  102.0 4.9 %copy-start.4 = (bf16[4,128,8,128]{1,3,2,0:T(8,128)(2,1)S(1)}, bf16[4,128,8,128]{1,3,2,0:T(8,128)(2,1)}, u32[]{:S(2)}) copy-start(bf16[4,128,8,128]{1,3,2,0:T(8,128)(2,1)} %copy.116) | copy-start | bytes 3145732
  102.0 4.9 %copy-start.12 = (f32[4,8,128,128]{2,3,1,0:T(8,128)S(1)}, f32[4,8,128,128]{2,3,1,0:T(8,128)}, u32[]{:S(2)}) copy-start(f32[4,8,128,128]{2,3,1,0:T(8,128)} %fusion.31) | copy-start | bytes 6291460
  106.9 2.0 copy-start.13
  123.0 2.1 copy-start.5
  125.1 1.0 copy-start.2
  126.1 5.0 %copy-start.9 = (f32[4,8,128,128]{3,2,1,0:T(8,128)}, f32[4,8,128,128]{3,2,1,0:T(8,128)S(1)}, u32[]{:S(2)}) copy-start(f32[4,8,128,128]{3,2,1,0:T(8,128)S(1)} %fusion.26) | copy-start | bytes 6291460
  131.2 2.4 %copy-start.1 = (bf16[64,8,8,128]{3,2,1,0:T(8,128)(2,1)S(1)}, bf16[64,8,8,128]{3,2,1,0:T(8,128)(2,1)}, u32[]{:S(2)}) copy-start(bf16[64,8,8,128]{3,2,1,0:T(8,128)(2,1)} %copy-done) | copy-start | bytes 3145732
  133.6 1.0 copy-start.17
  133.7 1.6 copy-start.3
  133.7 1.9 copy-start.14
  139.7 2.6 %copy-start.16 = (bf16[4,8,128,128]{3,2,1,0:T(8,128)(2,1)S(1)}, bf16[4,8,128,128]{3,2,1,0:T(8,128)(2,1)}, u32[]{:S(2)}) copy-start(bf16[4,8,128,128]{3,2,1,0:T(8,128)(2,1)} %copy-done.15) | copy-start | bytes 3145732
  142.3 2.2 copy-start.6
  142.3 2.2 copy-start.18
  202.5 8.4 %copy-start.10 = (f32[4,8,128,128]{3,2,1,0:T(8,128)S(1)}, f32[4,8,128,128]{3,2,1,0:T(8,128)}, u32[]{:S(2)}) copy-start(f32[4,8,128,128]{3,2,1,0:T(8,128)} %copy-done.9) | copy-start | bytes 6291460
  220.3 1.9 copy-start.11
Sparse Core Ops, SparseCore 0:
  17.3 76.2 all-gather.5
  131.2 71.2 all-gather.7
where the time goes:
time: 236 us; the launch traced here: 232 us
  waiting for transfers between devices  93.2 us (39%)
  matrix products  58.8 us (25%)
  blocking collectives  35.8 us (15%)
  local copies, waits for them, and re-layouts  24.2 us (10%)
  between operations  15.5 us (7%)
  other arithmetic  4.76 us (2%)
    all_gather x1, waiting for transfers between devices, shards(): shard_piece = lax.all_gather(shard_back[None], 'seq', axis=0, tiled=True)  55.7 us
    all_gather x1, waiting for transfers between devices, shards(): lax.all_gather(shard_state[None], 'seq', axis=0, tiled=True)  37.4 us
    unnamed x1, blocking collectives  23.5 us
    unnamed x56, local copies, waits for them, and re-layouts  13.1 us
    dot_general x1, matrix products, shards(): jnp.einsum('rh,rhde->hde', mixing, shard_piece, precision=highest)  8.35 us
    dot_general x1, matrix products, shards(): incoming = jnp.einsum('rh,rhde->hde', mixing, all_states, precision=highest)  8.35 us
    psum x1, blocking collectives, shards(): cross_total = lax.psum(cross_local, 'head')  6.61 us
    psum x1, blocking collectives, shards(): square_total = lax.psum(square, 'head')  5.64 us
  transfers between devices with their start and end apart: 2, of which 2 were waited for; matrix products, arithmetic and copies ran while one was open for 12% of the time, Pallas kernels for 0%

commit v1 on v0

v1 whole, which is shorter than its diff:
```python
import functools

import jax
import jax.numpy as jnp
from jax import lax
from jax.experimental import pallas as pl
from jax.experimental.pallas import tpu as pltpu
from jax.sharding import PartitionSpec as P

HEAD_COUNT = 32
DH = 128
BLOCK = 128
EPSILON = 1e-06

f32 = jnp.float32
bf16 = jnp.bfloat16


def dot(left, right, left_dim, right_dim):
    return lax.dot_general(
        left, right, (((left_dim,), (right_dim,)), ((), ())), preferred_element_type=f32
    )


def kernel(
    n_seq,
    n_head,
    q_hbm,
    k_hbm,
    v_hbm,
    g_hbm,
    ld_hbm,
    qo_hbm,
    ko_hbm,
    vo_hbm,
    q_ref,
    k_ref,
    v_ref,
    g_ref,
    ld_ref,
    within_ref,
    total_ref,
    dec_ref,
    shard_dec_ref,
    terms,
    mask_ref,
    grow_ref,
    end_ref,
    attn_ref,
    probs_ref,
    ag_ref,
    state_ref,
    ki_ref,
    vi_ref,
    slab,
    pair_in,
    chain_in,
    chain_out,
    pair_out,
    incoming,
    acc_ref,
    stat_out,
    stat_in,
    row_ref,
    q_out,
    k_out,
    v_out,
    load_sem,
    pair_send,
    pair_recv,
    chain_send,
    chain_recv,
    fin_send,
    fin_recv,
    stat_send,
    stat_recv,
    out_sem,
):
    heads = ld_ref.shape[0]
    blocks = ld_ref.shape[1] // BLOCK
    half = heads // 2
    groups = n_seq // 2
    rank = lax.axis_index("seq")
    col = lax.axis_index("head")
    x = lax.rem(rank, 2)
    z = rank // 2
    partner = rank + 1 - 2 * x

    loads = [
        pltpu.make_async_copy(src, dst, load_sem.at[at])
        for at, (src, dst) in enumerate(
            [(ld_hbm, ld_ref), (k_hbm, k_ref), (v_hbm, v_ref), (q_hbm, q_ref), (g_hbm, g_ref)]
        )
    ]
    for load in loads:
        load.start()

    barrier = pltpu.get_barrier_semaphore()
    pl.semaphore_signal(barrier, inc=1, device_id={"seq": partner})

    @pl.when(z > 0)
    def _():
        pl.semaphore_signal(barrier, inc=1, device_id={"seq": rank - 2})

    @pl.when(z < groups - 1)
    def _():
        pl.semaphore_signal(barrier, inc=1, device_id={"seq": rank + 2})

    for step in range(1, n_head):
        pl.semaphore_signal(barrier, inc=1, device_id={"head": lax.rem(col + step, n_head)})

    def head_at(i):
        return lax.rem(x * half + i, heads)

    def columns(i):
        return pl.ds(pl.multiple_of(head_at(i) * DH, DH), DH)

    def rows(n):
        return pl.ds(n * BLOCK, BLOCK)

    row_ids = lax.broadcasted_iota(jnp.int32, (BLOCK, BLOCK), 0)
    col_ids = lax.broadcasted_iota(jnp.int32, (BLOCK, BLOCK), 1)
    loads[0].wait()
    upto = (row_ids <= col_ids).astype(f32)
    shard_total = jnp.zeros((heads, BLOCK), f32)
    for n in range(blocks):
        within = lax.dot_general(
            ld_ref[:, rows(n)],
            upto,
            (((1,), (0,)), ((), ())),
            precision=lax.Precision.HIGHEST,
            preferred_element_type=f32,
        )
        total = jnp.broadcast_to(within[:, BLOCK - 1 : BLOCK], (heads, BLOCK))
        within_ref[n] = within
        total_ref[n] = total
        dec_ref[n] = jnp.exp(total)
        shard_total = shard_total + total
    shard_dec_ref[...] = jnp.exp(shard_total)
    loads[1].wait()
    loads[2].wait()

    def pair_copy(d, i):
        size = DH + 8 if d == 0 else DH
        j = i - half
        return pltpu.make_async_remote_copy(
            src_ref=slab.at[d, i, pl.ds(0, size)],
            dst_ref=pair_in.at[d, j, pl.ds(0, size)],
            send_sem=pair_send.at[d, j],
            recv_sem=pair_recv.at[d, j],
            device_id={"seq": partner},
        )

    def chain_copy(d, j):
        return pltpu.make_async_remote_copy(
            src_ref=chain_out.at[d, j],
            dst_ref=chain_in.at[d, j],
            send_sem=chain_send.at[d, j],
            recv_sem=chain_recv.at[d, j],
            device_id={"seq": rank + 2 - 4 * d},
        )

    def fin_copy(d, j):
        return pltpu.make_async_remote_copy(
            src_ref=pair_out.at[d, j],
            dst_ref=incoming.at[d, half + j],
            send_sem=fin_send.at[d, j],
            recv_sem=fin_recv.at[d, j],
            device_id={"seq": partner},
        )

    def forward_terms(i):
        h = head_at(i)
        at = columns(i)
        state = jnp.zeros((DH, DH), f32)
        for n in range(blocks):
            row = jnp.broadcast_to(within_ref[n, pl.ds(h, 1), :], (BLOCK, BLOCK))
            to_end = jnp.exp(total_ref[n, pl.ds(h, 1), :] - row.T)
            end_ref[i, rows(n)] = to_end
            scaled = (to_end * k_ref[rows(n), at].astype(f32)).astype(bf16)
            term = dot(scaled, v_ref[rows(n), at], 0, 0)
            terms[0, i, n] = term
            state = dec_ref[n, pl.ds(h, 1), :] * state + term
        slab[0, i, pl.ds(0, DH)] = state
        slab[0, i, pl.ds(DH, 8)] = jnp.broadcast_to(shard_dec_ref[pl.ds(h, 1), :], (8, DH))

    def forward_inside(i):
        h = head_at(i)
        at = columns(i)
        for n in range(blocks):
            row = jnp.broadcast_to(within_ref[n, pl.ds(h, 1), :], (BLOCK, BLOCK))
            column = row.T
            mask = jnp.where(
                row_ids >= col_ids, jnp.exp(jnp.minimum(column - row, 0.0)), 0.0
            )
            mask_ref[i, rows(n)] = mask
            grow_ref[i, rows(n)] = jnp.exp(column)
            probs = (dot(q_ref[rows(n), at], k_ref[rows(n), at], 1, 1) * mask).astype(bf16)
            probs_ref[i, rows(n)] = probs
            attn_ref[i, rows(n)] = dot(probs, v_ref[rows(n), at], 1, 0)

    def loop(low, high, body):
        def step(i, carry):
            body(i)
            return carry

        lax.fori_loop(low, high, step, 0)

    def scan(d):
        first = (x == 0) if d == 0 else (x == 1)
        at = z if d == 0 else groups - 1 - z

        def step(j):
            pair_copy(d, half + j).wait_recv()

            @pl.when(at > 0)
            def _():
                chain_copy(d, j).wait_recv()

            @pl.when(at == 0)
            def _():
                chain_in[d, j] = jnp.zeros((DH, DH), f32)

            mine, other = slab[d, j, pl.ds(0, DH)], pair_in[d, j, pl.ds(0, DH)]
            mine_dec, other_dec = slab[0, j, pl.ds(DH, 1)], pair_in[0, j, pl.ds(DH, 1)]
            first_state = jnp.where(first, mine, other)
            last_state = jnp.where(first, other, mine)
            first_dec = jnp.where(first, mine_dec, other_dec)
            last_dec = jnp.where(first, other_dec, mine_dec)
            before = chain_in[d, j]
            between = first_dec * before + first_state
            chain_out[d, j] = last_dec * between + last_state

            @pl.when(at < groups - 1)
            def _():
                chain_copy(d, j).start()

            incoming[d, j] = jnp.where(first, before, between)
            pair_out[d, j] = jnp.where(first, between, before)
            fin_copy(d, j).start()

        loop(0, half, step)

    n_peers = 1 + (z > 0).astype(jnp.int32) + (z < groups - 1).astype(jnp.int32) + n_head - 1
    pl.semaphore_wait(barrier, n_peers)

    def send_terms(i):
        forward_terms(i)
        pair_copy(0, i).start()

    loop(half, heads, send_terms)
    loop(0, half, forward_terms)
    loads[3].wait()
    ahead = (z * heads) // max(groups - 1, 1)
    loop(0, ahead, forward_inside)
    scan(0)
    loop(ahead, heads, forward_inside)
    loads[4].wait()

    acc_ref[...] = jnp.zeros_like(acc_ref)

    def complete(i):
        h = head_at(i)
        at = columns(i)
        state = incoming[0, i]
        for n in range(blocks):
            rounded = state.astype(bf16)
            state_ref[i, n] = rounded
            inter = dot(q_ref[rows(n), at], rounded, 1, 0)
            attn = attn_ref[i, rows(n)] + grow_ref[i, rows(n)] * inter
            attn_ref[i, rows(n)] = attn
            acc_ref[0, rows(n)] += attn * attn
            acc_ref[1, rows(n)] += attn * g_ref[rows(n), at].astype(f32)
            state = dec_ref[n, pl.ds(h, 1), :] * state + terms[0, i, n]

    def complete_foreign(i):
        fin_copy(0, i - half).wait_recv()
        complete(i)

    loop(0, half, complete)
    loop(half, heads, complete_foreign)

    for kind in range(2):
        for n in range(blocks):
            stat_out[pl.ds(kind * blocks + n, 1), :] = jnp.sum(
                acc_ref[kind, rows(n)].T, axis=0, keepdims=True
            )

    def stat_copy(step):
        return pltpu.make_async_remote_copy(
            src_ref=stat_out,
            dst_ref=stat_in.at[step - 1],
            send_sem=stat_send.at[step - 1],
            recv_sem=stat_recv.at[step - 1],
            device_id={"head": lax.rem(col + step, n_head)},
        )

    for step in range(1, n_head):
        stat_copy(step).start()
    stats = stat_out[...]
    for step in range(1, n_head):
        stat_copy(step).wait_recv()
        stats = stats + stat_in[step - 1]
    width = float(HEAD_COUNT * DH)
    inv_rms = lax.rsqrt(stats[:blocks] / width + EPSILON)
    coef = inv_rms * (inv_rms * stats[blocks:] / width)
    for n in range(blocks):
        row_ref[0, rows(n)] = jnp.broadcast_to(inv_rms[n : n + 1], (BLOCK, BLOCK)).T
        row_ref[1, rows(n)] = jnp.broadcast_to(coef[n : n + 1], (BLOCK, BLOCK)).T

    def back_terms(i):
        h = head_at(i)
        at = columns(i)
        state = jnp.zeros((DH, DH), f32)
        for n in reversed(range(blocks)):
            ag = (
                row_ref[0, rows(n)]
                * (g_ref[rows(n), at].astype(f32) - attn_ref[i, rows(n)] * row_ref[1, rows(n)])
            ).astype(bf16)
            ag_ref[i, rows(n)] = ag
            scaled = (grow_ref[i, rows(n)] * q_ref[rows(n), at].astype(f32)).astype(bf16)
            term = dot(scaled, ag, 0, 0)
            terms[1, i, n] = term
            state = dec_ref[n, pl.ds(h, 1), :] * state + term
        slab[1, i, pl.ds(0, DH)] = state

    def send_back_terms(i):
        back_terms(i)
        pair_copy(1, i).start()

    def out_copy(which, i):
        src, dst = ((q_out, qo_hbm), (k_out, ko_hbm), (v_out, vo_hbm))[which]
        return pltpu.make_async_copy(src.at[i], dst.at[:, columns(i)], out_sem.at[which, i])

    def back_inside(i):
        at = columns(i)
        for n in range(blocks):
            ag = ag_ref[i, rows(n)]
            grad = (dot(ag, v_ref[rows(n), at], 1, 1) * mask_ref[i, rows(n)]).astype(bf16)
            query = dot(grad, k_ref[rows(n), at], 1, 0)
            query = query + grow_ref[i, rows(n)] * dot(ag, state_ref[i, n], 1, 1)
            q_out[i, rows(n)] = query.astype(bf16)
            ki_ref[i, rows(n)] = dot(grad, q_ref[rows(n), at], 0, 0)
            vi_ref[i, rows(n)] = dot(probs_ref[i, rows(n)], ag, 0, 0)
        out_copy(0, i).start()

    loop(half, heads, send_back_terms)
    loop(0, half, back_terms)
    back_ahead = ((groups - 1 - z) * heads) // max(groups - 1, 1)
    loop(0, back_ahead, back_inside)
    scan(1)
    loop(back_ahead, heads, back_inside)

    def finish(i):
        h = head_at(i)
        at = columns(i)
        state = incoming[1, i]
        for n in reversed(range(blocks)):
            rounded = state.astype(bf16)
            to_end = end_ref[i, rows(n)]
            key = ki_ref[i, rows(n)] + to_end * dot(v_ref[rows(n), at], rounded, 1, 1)
            value = vi_ref[i, rows(n)] + to_end * dot(k_ref[rows(n), at], rounded, 1, 0)
            k_out[i, rows(n)] = key.astype(bf16)
            v_out[i, rows(n)] = value.astype(bf16)
            state = dec_ref[n, pl.ds(h, 1), :] * state + terms[1, i, n]
        out_copy(1, i).start()
        out_copy(2, i).start()

    def finish_foreign(i):
        fin_copy(1, i - half).wait_recv()
        finish(i)

    loop(0, half, finish)
    loop(half, heads, finish_foreign)

    for step in range(1, n_head):
        stat_copy(step).wait_send()
    for d in range(2):

        def drain(j):
            pair_copy(d, half + j).wait_send()
            fin_copy(d, j).wait_send()

            @pl.when((z < groups - 1) if d == 0 else (z > 0))
            def _():
                chain_copy(d, j).wait_send()

        loop(0, half, drain)

    def drain_out(i):
        for which in range(3):
            out_copy(which, i).wait()

    loop(0, heads, drain_out)


def solution(mesh):
    n_seq, n_head = mesh.shape["seq"], mesh.shape["head"]

    def shards(queries, key_rows, value_rows, out_grad, log_decay):
        tokens, width = queries.shape
        heads = log_decay.shape[0]
        blocks = tokens // BLOCK
        half = heads // 2
        full = (heads, tokens, DH)
        dma = pltpu.SemaphoreType.DMA
        scratch = [
            pltpu.VMEM((tokens, width), bf16),
            pltpu.VMEM((tokens, width), bf16),
            pltpu.VMEM((tokens, width), bf16),
            pltpu.VMEM((tokens, width), bf16),
            pltpu.VMEM((heads, tokens), f32),
            pltpu.VMEM((blocks, heads, BLOCK), f32),
            pltpu.VMEM((blocks, heads, BLOCK), f32),
            pltpu.VMEM((blocks, heads, BLOCK), f32),
            pltpu.VMEM((heads, BLOCK), f32),
            pltpu.VMEM((2, heads, blocks, DH, DH), f32),
            pltpu.VMEM(full, f32),
            pltpu.VMEM(full, f32),
            pltpu.VMEM(full, f32),
            pltpu.VMEM(full, f32),
            pltpu.VMEM(full, bf16),
            pltpu.VMEM(full, bf16),
            pltpu.VMEM((heads, blocks, DH, DH), bf16),
            pltpu.VMEM(full, f32),
            pltpu.VMEM(full, f32),
            pltpu.VMEM((2, heads, DH + 8, DH), f32),
            pltpu.VMEM((2, half, DH + 8, DH), f32),
            pltpu.VMEM((2, half, DH, DH), f32),
            pltpu.VMEM((2, half, DH, DH), f32),
            pltpu.VMEM((2, half, DH, DH), f32),
            pltpu.VMEM((2, heads, DH, DH), f32),
            pltpu.VMEM((2, tokens, DH), f32),
            pltpu.VMEM((2 * blocks, BLOCK), f32),
            pltpu.VMEM((n_head - 1, 2 * blocks, BLOCK), f32),
            pltpu.VMEM((2, tokens, DH), f32),
            pltpu.VMEM(full, bf16),
            pltpu.VMEM(full, bf16),
            pltpu.VMEM(full, bf16),
            dma((5,)),
            dma((2, half)),
            dma((2, half)),
            dma((2, half)),
            dma((2, half)),
            dma((2, half)),
            dma((2, half)),
            dma((n_head - 1,)),
            dma((n_head - 1,)),
            dma((3, heads)),
        ]
        anywhere = pl.BlockSpec(memory_space=pl.ANY)
        return pl.pallas_call(
            functools.partial(kernel, n_seq, n_head),
            out_shape=[jax.ShapeDtypeStruct((tokens, width), bf16)] * 3,
            in_specs=[anywhere] * 5,
            out_specs=[anywhere] * 3,
            scratch_shapes=scratch,
            compiler_params=pltpu.CompilerParams(
                collective_id=0,
                has_side_effects=True,
                vmem_limit_bytes=48 * 1024 * 1024,
            ),
            name="lightning",
        )(queries, key_rows, value_rows, out_grad, log_decay)

    return jax.shard_map(
        shards,
        mesh=mesh,
        in_specs=(
            P("seq", "head"),
            P("seq", "head"),
            P("seq", "head"),
            P("seq", "head"),
            P("head", "seq"),
        ),
        out_specs=(P("seq", "head"), P("seq", "head"), P("seq", "head")),
        check_vma=False,
    )
```

time: 236 us -> 58.6 us (0.25); the launches traced: 232 us -> 58.3 us
  waiting for transfers between devices: 93.2 us -> 0 us
  matrix products: 58.8 us -> 0 us
  Pallas kernels: 0 us -> 51.6 us
  blocking collectives: 35.8 us -> 0 us
  local copies, waits for them, and re-layouts: 24.2 us -> 6.07 us
  between operations: 15.5 us -> 0.65 us
  other arithmetic: 4.76 us -> 0 us
    all_gather x2 -> x0, waiting for transfers between devices: 93.1 us -> none  [the longest x1 55.7 us: shards(): shard_piece = lax.all_gather(shard_back[None], 'seq', axis=0, tiled=True)]
    dot_general x18 -> x0, matrix products: 58.8 us -> none  [the longest x1 8.35 us: shards(): jnp.einsum('rh,rhde->hde', mixing, shard_piece, precision=highest)]
    pallas_call x0 -> x1, Pallas kernels: none -> 51.6 us  [shards(): pl.pallas_call(functools.partial(kernel, n_seq, n_head), out_shape=[jax.S...]
    unnamed x1 -> x0, blocking collectives: 23.5 us -> none
    psum x2 -> x0, blocking collectives: 12.2 us -> none  [the longest x1 6.61 us: shards(): cross_total = lax.psum(cross_local, 'head')]
    convert_element_type x5 -> x0, local copies, waits for them, and re-layouts: 7.64 us -> none  [the longest x1 2.63 us: shards(): query_gradient.reshape(tok_rows, row_width).astype(jnp.bfloat16)]
    unnamed x56 -> x9, local copies, waits for them, and re-layouts: 13.1 us -> 6.07 us
    reshape x2 -> x0, local copies, waits for them, and re-layouts: 2.38 us -> none  [the longest x1 1.46 us: shards(): query_block_rows = queries.reshape(block_shape)]
  transfers between devices with their start and end apart: 2 -> 0, of which waited for: 2 -> 0; matrix products, arithmetic and copies ran while one was open for 12% -> 0% of each run, Pallas kernels for 0% -> 0%
where the time goes in v1:
time: 58.6 us; the launch traced here: 58.3 us
  Pallas kernels  51.6 us (88%)
  local copies, waits for them, and re-layouts  6.07 us (10%)
  between operations  0.65 us (1%)
    pallas_call x1, Pallas kernels, shards(): pl.pallas_call(functools.partial(kernel, n_seq, n_head), out_shape=[jax.S...  51.6 us
    unnamed x9, local copies, waits for them, and re-layouts  6.07 us

profile of v1, /device:TPU:0, one launch (start us, length us, event | category | flops | bytes accessed | tf_op | source)
XLA Modules:
  0.0 58.3 jit_solution(9583471989563366756)
XLA Ops:
  0.6 0.0 copy-start
  0.6 1.2 %copy-done = bf16[512,1024]{1,0:T(8,128)(2,1)S(1)} copy-done((bf16[512,1024]{1,0:T(8,128)(2,1)S(1)}, bf16[512,1024]{1,0:T(8,128)(2,1)}, u32[]{:S(2)}) %copy-start) | copy-done | bytes 1048600
  1.9 0.0 copy-start.1
  1.9 1.2 %copy-done.1 = bf16[512,1024]{1,0:T(8,128)(2,1)S(1)} copy-done((bf16[512,1024]{1,0:T(8,128)(2,1)S(1)}, bf16[512,1024]{1,0:T(8,128)(2,1)}, u32[]{:S(2)}) %copy-start.1) | copy-done | bytes 1048600
  3.1 0.0 copy-start.2
  3.1 0.7 %copy-done.2 = f32[8,512]{1,0:T(8,128)S(1)} copy-done((f32[8,512]{1,0:T(8,128)S(1)}, f32[8,512]{1,0:T(8,128)}, u32[]{:S(2)}) %copy-start.2) | copy-done | bytes 16408
  3.8 51.6 %lightning.1 = (bf16[512,1024]{1,0:T(8,128)(2,1)S(1)}, bf16[512,1024]{1,0:T(8,128)(2,1)S(1)}, bf16[512,1024]{1,0:T(8,128)(2,1)S(1)}) custom-call(bf16[512,1024]{1,0:T(8,128)(2,1)S(1)} %copy-done, bf16[512,1024]{1,0:T(8,128)(2,1)S(1)} %copy-done.1, bf16[512,1024]{1,0:T(8,128)(2,1)} %v_hbm.1, bf16[512,1024]{1,0:T(8,128)(2,1)} %g_hbm.1, f32[8,512]{1,0:T(8,128)S(1)} %copy-done.2), custom_call_target="tpu_custom_call" | custom-call | tf_op jit(solution)/shard_map/lightning/pallas_call | solution.py:452
  55.4 1.0 %copy.11 = bf16[512,1024]{1,0:T(8,128)(2,1)} copy(bf16[512,1024]{1,0:T(8,128)(2,1)S(1)} %get-tuple-element.6) | data formatting | bytes 2097152
  56.4 1.0 %copy.12 = bf16[512,1024]{1,0:T(8,128)(2,1)} copy(bf16[512,1024]{1,0:T(8,128)(2,1)S(1)} %get-tuple-element.7) | data formatting | bytes 2097152
  57.3 1.0 %copy.13 = bf16[512,1024]{1,0:T(8,128)(2,1)} copy(bf16[512,1024]{1,0:T(8,128)(2,1)S(1)} %get-tuple-element.8) | data formatting | bytes 2097152
Async XLA Ops:
  0.6 1.2 %copy-start = (bf16[512,1024]{1,0:T(8,128)(2,1)S(1)}, bf16[512,1024]{1,0:T(8,128)(2,1)}, u32[]{:S(2)}) copy-start(bf16[512,1024]{1,0:T(8,128)(2,1)} %q_hbm.1) | copy-start | bytes 3145732
  1.9 1.2 %copy-start.1 = (bf16[512,1024]{1,0:T(8,128)(2,1)S(1)}, bf16[512,1024]{1,0:T(8,128)(2,1)}, u32[]{:S(2)}) copy-start(bf16[512,1024]{1,0:T(8,128)(2,1)} %k_hbm.1) | copy-start | bytes 3145732
  3.1 0.7 %copy-start.2 = (f32[8,512]{1,0:T(8,128)S(1)}, f32[8,512]{1,0:T(8,128)}, u32[]{:S(2)}) copy-start(f32[8,512]{1,0:T(8,128)} %ld_hbm.1) | copy-start | bytes 49156

commit v2 on v1

--- a/solution.py
+++ b/solution.py
@@ -10,6 +10,9 @@
 HEAD_COUNT = 32
 DH = 128
 BLOCK = 128
+CUTS = 2
+PIECE = DH // CUTS
+VMEM_LIMIT = 61 * 1024 * 1024
 EPSILON = 1e-06
 
 f32 = jnp.float32
@@ -140,32 +143,32 @@
     loads[1].wait()
     loads[2].wait()
 
-    def pair_copy(d, i):
-        size = DH + 8 if d == 0 else DH
+    def pair_copy(d, i, c):
+        size = PIECE + 8 if d == 0 else PIECE
         j = i - half
         return pltpu.make_async_remote_copy(
-            src_ref=slab.at[d, i, pl.ds(0, size)],
-            dst_ref=pair_in.at[d, j, pl.ds(0, size)],
-            send_sem=pair_send.at[d, j],
-            recv_sem=pair_recv.at[d, j],
+            src_ref=slab.at[d, i, c, pl.ds(0, size)],
+            dst_ref=pair_in.at[d, j, c, pl.ds(0, size)],
+            send_sem=pair_send.at[d, j, c],
+            recv_sem=pair_recv.at[d, j, c],
             device_id={"seq": partner},
         )
 
-    def chain_copy(d, j):
+    def chain_copy(d, j, c):
         return pltpu.make_async_remote_copy(
-            src_ref=chain_out.at[d, j],
-            dst_ref=chain_in.at[d, j],
-            send_sem=chain_send.at[d, j],
-            recv_sem=chain_recv.at[d, j],
+            src_ref=chain_out.at[d, j, c],
+            dst_ref=chain_in.at[d, j, c],
+            send_sem=chain_send.at[d, j, c],
+            recv_sem=chain_recv.at[d, j, c],
             device_id={"seq": rank + 2 - 4 * d},
         )
 
-    def fin_copy(d, j):
+    def fin_copy(d, j, c):
         return pltpu.make_async_remote_copy(
-            src_ref=pair_out.at[d, j],
-            dst_ref=incoming.at[d, half + j],
-            send_sem=fin_send.at[d, j],
-            recv_sem=fin_recv.at[d, j],
+            src_ref=pair_out.at[d, j, c],
+            dst_ref=incoming.at[d, half + j, pl.ds(c * PIECE, PIECE)],
+            send_sem=fin_send.at[d, j, c],
+            recv_sem=fin_recv.at[d, j, c],
             device_id={"seq": partner},
         )
 
@@ -181,8 +184,11 @@
             term = dot(scaled, v_ref[rows(n), at], 0, 0)
             terms[0, i, n] = term
             state = dec_ref[n, pl.ds(h, 1), :] * state + term
-        slab[0, i, pl.ds(0, DH)] = state
-        slab[0, i, pl.ds(DH, 8)] = jnp.broadcast_to(shard_dec_ref[pl.ds(h, 1), :], (8, DH))
+        for c in range(CUTS):
+            slab[0, i, c, pl.ds(0, PIECE)] = state[c * PIECE : (c + 1) * PIECE]
+            slab[0, i, c, pl.ds(PIECE, 8)] = jnp.broadcast_to(
+                shard_dec_ref[pl.ds(h, 1), :], (8, DH)
+            )
 
     def forward_inside(i):
         h = head_at(i)
@@ -206,38 +212,41 @@
 
         lax.fori_loop(low, high, step, 0)
 
-    def scan(d):
+    def scan(d, unit):
         first = (x == 0) if d == 0 else (x == 1)
         at = z if d == 0 else groups - 1 - z
 
         def step(j):
-            pair_copy(d, half + j).wait_recv()
-
-            @pl.when(at > 0)
-            def _():
-                chain_copy(d, j).wait_recv()
-
-            @pl.when(at == 0)
-            def _():
-                chain_in[d, j] = jnp.zeros((DH, DH), f32)
-
-            mine, other = slab[d, j, pl.ds(0, DH)], pair_in[d, j, pl.ds(0, DH)]
-            mine_dec, other_dec = slab[0, j, pl.ds(DH, 1)], pair_in[0, j, pl.ds(DH, 1)]
-            first_state = jnp.where(first, mine, other)
-            last_state = jnp.where(first, other, mine)
-            first_dec = jnp.where(first, mine_dec, other_dec)
-            last_dec = jnp.where(first, other_dec, mine_dec)
-            before = chain_in[d, j]
-            between = first_dec * before + first_state
-            chain_out[d, j] = last_dec * between + last_state
-
-            @pl.when(at < groups - 1)
-            def _():
-                chain_copy(d, j).start()
-
-            incoming[d, j] = jnp.where(first, before, between)
-            pair_out[d, j] = jnp.where(first, between, before)
-            fin_copy(d, j).start()
+            for c in range(CUTS):
+                pair_copy(d, half + j, c).wait_recv()
+
+                @pl.when(at > 0)
+                def _():
+                    chain_copy(d, j, c).wait_recv()
+
+                @pl.when(at == 0)
+                def _():
+                    chain_in[d, j, c] = jnp.zeros((PIECE, DH), f32)
+
+                mine, other = slab[d, j, c, pl.ds(0, PIECE)], pair_in[d, j, c, pl.ds(0, PIECE)]
+                mine_dec = slab[0, j, c, pl.ds(PIECE, 1)]
+                other_dec = pair_in[0, j, c, pl.ds(PIECE, 1)]
+                first_state = jnp.where(first, mine, other)
+                last_state = jnp.where(first, other, mine)
+                first_dec = jnp.where(first, mine_dec, other_dec)
+                last_dec = jnp.where(first, other_dec, mine_dec)
+                before = chain_in[d, j, c]
+                between = first_dec * before + first_state
+                chain_out[d, j, c] = last_dec * between + last_state
+
+                @pl.when(at < groups - 1)
+                def _():
+                    chain_copy(d, j, c).start()
+
+                incoming[d, j, pl.ds(c * PIECE, PIECE)] = jnp.where(first, before, between)
+                pair_out[d, j, c] = jnp.where(first, between, before)
+                fin_copy(d, j, c).start()
+            unit(j)
 
         loop(0, half, step)
 
@@ -246,17 +255,12 @@
 
     def send_terms(i):
         forward_terms(i)
-        pair_copy(0, i).start()
+        for c in range(CUTS):
+            pair_copy(0, i, c).start()
 
     loop(half, heads, send_terms)
     loop(0, half, forward_terms)
     loads[3].wait()
-    ahead = (z * heads) // max(groups - 1, 1)
-    loop(0, ahead, forward_inside)
-    scan(0)
-    loop(ahead, heads, forward_inside)
-    loads[4].wait()
-
     acc_ref[...] = jnp.zeros_like(acc_ref)
 
     def complete(i):
@@ -274,11 +278,32 @@
             state = dec_ref[n, pl.ds(h, 1), :] * state + terms[0, i, n]
 
     def complete_foreign(i):
-        fin_copy(0, i - half).wait_recv()
+        for c in range(CUTS):
+            fin_copy(0, i - half, c).wait_recv()
         complete(i)
 
-    loop(0, half, complete)
-    loop(half, heads, complete_foreign)
+    def units(ahead, inside, after):
+        def unit(j):
+            @pl.when(ahead + j < heads)
+            def _():
+                inside(ahead + j)
+
+            @pl.when(ahead + j >= heads)
+            def _():
+                after(ahead + j - heads)
+
+        return unit
+
+    def run(d, at, inside, after, after_foreign):
+        ahead = (at * heads) // max(groups - 1, 1)
+        loop(0, ahead, inside)
+        scan(d, units(ahead, inside, after))
+        loop(ahead + half, heads, inside)
+        loop(jnp.maximum(ahead + half - heads, 0), half, after)
+        loop(half, heads, after_foreign)
+
+    loads[4].wait()
+    run(0, z, forward_inside, complete, complete_foreign)
 
     for kind in range(2):
         for n in range(blocks):
@@ -322,11 +347,13 @@
             term = dot(scaled, ag, 0, 0)
             terms[1, i, n] = term
             state = dec_ref[n, pl.ds(h, 1), :] * state + term
-        slab[1, i, pl.ds(0, DH)] = state
+        for c in range(CUTS):
+            slab[1, i, c, pl.ds(0, PIECE)] = state[c * PIECE : (c + 1) * PIECE]
 
     def send_back_terms(i):
         back_terms(i)
-        pair_copy(1, i).start()
+        for c in range(CUTS):
+            pair_copy(1, i, c).start()
 
     def out_copy(which, i):
         src, dst = ((q_out, qo_hbm), (k_out, ko_hbm), (v_out, vo_hbm))[which]
@@ -346,10 +373,6 @@
 
     loop(half, heads, send_back_terms)
     loop(0, half, back_terms)
-    back_ahead = ((groups - 1 - z) * heads) // max(groups - 1, 1)
-    loop(0, back_ahead, back_inside)
-    scan(1)
-    loop(back_ahead, heads, back_inside)
 
     def finish(i):
         h = head_at(i)
@@ -367,23 +390,24 @@
         out_copy(2, i).start()
 
     def finish_foreign(i):
-        fin_copy(1, i - half).wait_recv()
+        for c in range(CUTS):
+            fin_copy(1, i - half, c).wait_recv()
         finish(i)
 
-    loop(0, half, finish)
-    loop(half, heads, finish_foreign)
+    run(1, groups - 1 - z, back_inside, finish, finish_foreign)
 
     for step in range(1, n_head):
         stat_copy(step).wait_send()
     for d in range(2):
 
         def drain(j):
-            pair_copy(d, half + j).wait_send()
-            fin_copy(d, j).wait_send()
-
-            @pl.when((z < groups - 1) if d == 0 else (z > 0))
-            def _():
-                chain_copy(d, j).wait_send()
+            for c in range(CUTS):
+                pair_copy(d, half + j, c).wait_send()
+                fin_copy(d, j, c).wait_send()
+
+                @pl.when((z < groups - 1) if d == 0 else (z > 0))
+                def _():
+                    chain_copy(d, j, c).wait_send()
 
         loop(0, half, drain)
 
@@ -392,6 +416,20 @@
             out_copy(which, i).wait()
 
     loop(0, heads, drain_out)
+
+
+def write_out(q_in, k_in, v_in, q_hbm, k_hbm, v_hbm, sem):
+    copies = [
+        pltpu.make_async_copy(
+            src.at[pl.ds(n * BLOCK, BLOCK)], dst.at[pl.ds(n * BLOCK, BLOCK)], sem.at[at, n]
+        )
+        for at, (src, dst) in enumerate([(q_in, q_hbm), (k_in, k_hbm), (v_in, v_hbm)])
+        for n in range(q_in.shape[0] // BLOCK)
+    ]
+    for copy in copies:
+        copy.start()
+    for copy in copies:
+        copy.wait()
 
 
 def solution(mesh):
@@ -424,11 +462,11 @@
             pltpu.VMEM((heads, blocks, DH, DH), bf16),
             pltpu.VMEM(full, f32),
             pltpu.VMEM(full, f32),
-            pltpu.VMEM((2, heads, DH + 8, DH), f32),
-            pltpu.VMEM((2, half, DH + 8, DH), f32),
-            pltpu.VMEM((2, half, DH, DH), f32),
-            pltpu.VMEM((2, half, DH, DH), f32),
-            pltpu.VMEM((2, half, DH, DH), f32),
+            pltpu.VMEM((2, heads, CUTS, PIECE + 8, DH), f32),
+            pltpu.VMEM((2, half, CUTS, PIECE + 8, DH), f32),
+            pltpu.VMEM((2, half, CUTS, PIECE, DH), f32),
+            pltpu.VMEM((2, half, CUTS, PIECE, DH), f32),
+            pltpu.VMEM((2, half, CUTS, PIECE, DH), f32),
             pltpu.VMEM((2, heads, DH, DH), f32),
             pltpu.VMEM((2, tokens, DH), f32),
             pltpu.VMEM((2 * blocks, BLOCK), f32),
@@ -438,30 +476,40 @@
             pltpu.VMEM(full, bf16),
             pltpu.VMEM(full, bf16),
             dma((5,)),
-            dma((2, half)),
-            dma((2, half)),
-            dma((2, half)),
-            dma((2, half)),
-            dma((2, half)),
-            dma((2, half)),
+            dma((2, half, CUTS)),
+            dma((2, half, CUTS)),
+            dma((2, half, CUTS)),
+            dma((2, half, CUTS)),
+            dma((2, half, CUTS)),
+            dma((2, half, CUTS)),
             dma((n_head - 1,)),
             dma((n_head - 1,)),
             dma((3, heads)),
         ]
         anywhere = pl.BlockSpec(memory_space=pl.ANY)
-        return pl.pallas_call(
+        in_hbm = pl.BlockSpec(memory_space=pltpu.HBM)
+        results = pl.pallas_call(
             functools.partial(kernel, n_seq, n_head),
             out_shape=[jax.ShapeDtypeStruct((tokens, width), bf16)] * 3,
-            in_specs=[anywhere] * 5,
+            in_specs=[in_hbm] * 5,
             out_specs=[anywhere] * 3,
             scratch_shapes=scratch,
             compiler_params=pltpu.CompilerParams(
                 collective_id=0,
                 has_side_effects=True,
-                vmem_limit_bytes=48 * 1024 * 1024,
+                vmem_limit_bytes=VMEM_LIMIT,
             ),
             name="lightning",
         )(queries, key_rows, value_rows, out_grad, log_decay)
+        return pl.pallas_call(
+            write_out,
+            out_shape=[jax.ShapeDtypeStruct((tokens, width), bf16)] * 3,
+            in_specs=[anywhere] * 3,
+            out_specs=[in_hbm] * 3,
+            scratch_shapes=[dma((3, blocks))],
+            compiler_params=pltpu.CompilerParams(vmem_limit_bytes=VMEM_LIMIT),
+            name="write_out",
+        )(*results)
 
     return jax.shard_map(
         shards,

time: 58.6 us -> 148 us (2.53)
  Pallas kernels: 51.6 us -> 147 us
  local copies, waits for them, and re-layouts: 6.07 us -> 0 us
    pallas_call x0 -> x1, Pallas kernels: none -> 96.5 us  [shards(): pl.pallas_call(write_out, out_shape=[jax.ShapeDtypeStruct((tokens, width)...]
    unnamed x9 -> x0, local copies, waits for them, and re-layouts: 6.07 us -> none
where the time goes in v2:
time: 148 us
  Pallas kernels  147 us (99%)
    pallas_call x1, Pallas kernels, shards(): pl.pallas_call(write_out, out_shape=[jax.ShapeDtypeStruct((tokens, width)...  96.5 us
    pallas_call x1, Pallas kernels, shards(): pl.pallas_call(functools.partial(kernel, n_seq, n_head), out_shape=[jax.S...  50.4 us

profile of v2, /device:TPU:0, one launch (start us, length us, event | category | flops | bytes accessed | tf_op | source)
XLA Modules:
  0.0 147.5 jit_solution(6639803852131409698)
XLA Ops:
  0.6 50.4 %lightning.1 = (bf16[512,1024]{1,0:T(8,128)(2,1)}, bf16[512,1024]{1,0:T(8,128)(2,1)}, bf16[512,1024]{1,0:T(8,128)(2,1)}) custom-call(bf16[512,1024]{1,0:T(8,128)(2,1)} %q_hbm.1, bf16[512,1024]{1,0:T(8,128)(2,1)} %k_hbm.1, bf16[512,1024]{1,0:T(8,128)(2,1)} %v_hbm.1, bf16[512,1024]{1,0:T(8,128)(2,1)} %g_hbm.1, f32[8,512]{1,0:T(8,128)} %ld_hbm.1), custom_call_target="tpu_custom_call" | custom-call | tf_op jit(solution)/shard_map/lightning/pallas_call | solution.py:491
  51.0 96.5 %write_out.1 = (bf16[512,1024]{1,0:T(8,128)(2,1)}, bf16[512,1024]{1,0:T(8,128)(2,1)}, bf16[512,1024]{1,0:T(8,128)(2,1)}) custom-call(bf16[512,1024]{1,0:T(8,128)(2,1)} %get-tuple-element.6.q_in, bf16[512,1024]{1,0:T(8,128)(2,1)} %get-tuple-element.7.k_in, bf16[512,1024]{1,0:T(8,128)(2,1)} %get-tuple-element.8.v_in), custom_call_target="tpu_custom_call" | custom-call | tf_op jit(solution)/shard_map/write_out/pallas_call | solution.py:504

commit v3 on v2

--- a/solution.py
+++ b/solution.py
@@ -42,6 +42,7 @@
     g_ref,
     ld_ref,
     within_ref,
+    column_ref,
     total_ref,
     dec_ref,
     shard_dec_ref,
@@ -89,10 +90,21 @@
     z = rank // 2
     partner = rank + 1 - 2 * x
 
+    half_width = half * DH
+    near = pl.ds(pl.multiple_of(x * half_width, DH), half_width)
+    far = pl.ds(pl.multiple_of((1 - x) * half_width, DH), half_width)
     loads = [
         pltpu.make_async_copy(src, dst, load_sem.at[at])
         for at, (src, dst) in enumerate(
-            [(ld_hbm, ld_ref), (k_hbm, k_ref), (v_hbm, v_ref), (q_hbm, q_ref), (g_hbm, g_ref)]
+            [
+                (ld_hbm, ld_ref),
+                (k_hbm.at[:, far], k_ref.at[:, far]),
+                (v_hbm.at[:, far], v_ref.at[:, far]),
+                (k_hbm.at[:, near], k_ref.at[:, near]),
+                (v_hbm.at[:, near], v_ref.at[:, near]),
+                (q_hbm, q_ref),
+                (g_hbm, g_ref),
+            ]
         )
     ]
     for load in loads:
@@ -125,6 +137,7 @@
     col_ids = lax.broadcasted_iota(jnp.int32, (BLOCK, BLOCK), 1)
     loads[0].wait()
     upto = (row_ids <= col_ids).astype(f32)
+    since = (row_ids >= col_ids).astype(f32)
     shard_total = jnp.zeros((heads, BLOCK), f32)
     for n in range(blocks):
         within = lax.dot_general(
@@ -135,6 +148,15 @@
             preferred_element_type=f32,
         )
         total = jnp.broadcast_to(within[:, BLOCK - 1 : BLOCK], (heads, BLOCK))
+        by_column = lax.dot_general(
+            since,
+            ld_ref[:, rows(n)],
+            (((1,), (1,)), ((), ())),
+            precision=lax.Precision.HIGHEST,
+            preferred_element_type=f32,
+        )
+        for h in range(heads):
+            column_ref[h, rows(n)] = jnp.broadcast_to(by_column[:, h : h + 1], (BLOCK, BLOCK))
         within_ref[n] = within
         total_ref[n] = total
         dec_ref[n] = jnp.exp(total)
@@ -177,8 +199,7 @@
         at = columns(i)
         state = jnp.zeros((DH, DH), f32)
         for n in range(blocks):
-            row = jnp.broadcast_to(within_ref[n, pl.ds(h, 1), :], (BLOCK, BLOCK))
-            to_end = jnp.exp(total_ref[n, pl.ds(h, 1), :] - row.T)
+            to_end = jnp.exp(total_ref[n, pl.ds(h, 1), :] - column_ref[h, rows(n)])
             end_ref[i, rows(n)] = to_end
             scaled = (to_end * k_ref[rows(n), at].astype(f32)).astype(bf16)
             term = dot(scaled, v_ref[rows(n), at], 0, 0)
@@ -194,8 +215,8 @@
         h = head_at(i)
         at = columns(i)
         for n in range(blocks):
-            row = jnp.broadcast_to(within_ref[n, pl.ds(h, 1), :], (BLOCK, BLOCK))
-            column = row.T
+            row = within_ref[n, pl.ds(h, 1), :]
+            column = column_ref[h, rows(n)]
             mask = jnp.where(
                 row_ids >= col_ids, jnp.exp(jnp.minimum(column - row, 0.0)), 0.0
             )
@@ -259,8 +280,10 @@
             pair_copy(0, i, c).start()
 
     loop(half, heads, send_terms)
+    loads[3].wait()
+    loads[4].wait()
     loop(0, half, forward_terms)
-    loads[3].wait()
+    loads[5].wait()
     acc_ref[...] = jnp.zeros_like(acc_ref)
 
     def complete(i):
@@ -302,14 +325,15 @@
         loop(jnp.maximum(ahead + half - heads, 0), half, after)
         loop(half, heads, after_foreign)
 
-    loads[4].wait()
+    loads[6].wait()
     run(0, z, forward_inside, complete, complete_foreign)
 
-    for kind in range(2):
-        for n in range(blocks):
-            stat_out[pl.ds(kind * blocks + n, 1), :] = jnp.sum(
-                acc_ref[kind, rows(n)].T, axis=0, keepdims=True
-            )
+    sums = [
+        jnp.sum(acc_ref[kind, rows(n)], axis=1, keepdims=True)
+        for kind in range(2)
+        for n in range(blocks)
+    ]
+    stat_out[...] = jnp.concatenate(sums, axis=1).T
 
     def stat_copy(step):
         return pltpu.make_async_remote_copy(
@@ -329,9 +353,11 @@
     width = float(HEAD_COUNT * DH)
     inv_rms = lax.rsqrt(stats[:blocks] / width + EPSILON)
     coef = inv_rms * (inv_rms * stats[blocks:] / width)
-    for n in range(blocks):
-        row_ref[0, rows(n)] = jnp.broadcast_to(inv_rms[n : n + 1], (BLOCK, BLOCK)).T
-        row_ref[1, rows(n)] = jnp.broadcast_to(coef[n : n + 1], (BLOCK, BLOCK)).T
+    scales = jnp.concatenate([inv_rms, coef], axis=0).T
+    for kind in range(2):
+        for n in range(blocks):
+            at = kind * blocks + n
+            row_ref[kind, rows(n)] = jnp.broadcast_to(scales[:, at : at + 1], (BLOCK, BLOCK))
 
     def back_terms(i):
         h = head_at(i)
@@ -418,18 +444,21 @@
     loop(0, heads, drain_out)
 
 
-def write_out(q_in, k_in, v_in, q_hbm, k_hbm, v_hbm, sem):
-    copies = [
-        pltpu.make_async_copy(
-            src.at[pl.ds(n * BLOCK, BLOCK)], dst.at[pl.ds(n * BLOCK, BLOCK)], sem.at[at, n]
-        )
-        for at, (src, dst) in enumerate([(q_in, q_hbm), (k_in, k_hbm), (v_in, v_hbm)])
-        for n in range(q_in.shape[0] // BLOCK)
-    ]
-    for copy in copies:
-        copy.start()
-    for copy in copies:
-        copy.wait()
+def write_out(q_in, k_in, v_in, q_hbm, k_hbm, v_hbm, stage, in_sem, out_sem):
+    reads, writes = [], []
+    for at, (src, dst) in enumerate([(q_in, q_hbm), (k_in, k_hbm), (v_in, v_hbm)]):
+        for n in range(src.shape[0] // BLOCK):
+            part = pl.ds(n * BLOCK, BLOCK)
+            held = stage.at[at, part]
+            reads.append(pltpu.make_async_copy(src.at[part], held, in_sem.at[at, n]))
+            writes.append(pltpu.make_async_copy(held, dst.at[part], out_sem.at[at, n]))
+    for read in reads:
+        read.start()
+    for read, write in zip(reads, writes):
+        read.wait()
+        write.start()
+    for write in writes:
+        write.wait()
 
 
 def solution(mesh):
@@ -449,6 +478,7 @@
             pltpu.VMEM((tokens, width), bf16),
             pltpu.VMEM((heads, tokens), f32),
             pltpu.VMEM((blocks, heads, BLOCK), f32),
+            pltpu.VMEM(full, f32),
             pltpu.VMEM((blocks, heads, BLOCK), f32),
             pltpu.VMEM((blocks, heads, BLOCK), f32),
             pltpu.VMEM((heads, BLOCK), f32),
@@ -475,7 +505,7 @@
             pltpu.VMEM(full, bf16),
             pltpu.VMEM(full, bf16),
             pltpu.VMEM(full, bf16),
-            dma((5,)),
+            dma((7,)),
             dma((2, half, CUTS)),
             dma((2, half, CUTS)),
             dma((2, half, CUTS)),
@@ -506,7 +536,11 @@
             out_shape=[jax.ShapeDtypeStruct((tokens, width), bf16)] * 3,
             in_specs=[anywhere] * 3,
             out_specs=[in_hbm] * 3,
-            scratch_shapes=[dma((3, blocks))],
+            scratch_shapes=[
+                pltpu.VMEM((3, tokens, width), bf16),
+                dma((3, blocks)),
+                dma((3, blocks)),
+            ],
             compiler_params=pltpu.CompilerParams(vmem_limit_bytes=VMEM_LIMIT),
             name="write_out",
         )(*results)

time: 148 us -> 54.3 us (0.37)
  Pallas kernels: 147 us -> 53.4 us
    pallas_call x1, Pallas kernels: 96.5 us -> 2.81 us  [shards(): pl.pallas_call(write_out, out_shape=[jax.ShapeDtypeStruct((tokens, width)...]
where the time goes in v3:
time: 54.3 us; the launch traced here: 54 us
  Pallas kernels  53.4 us (98%)
  between operations  0.64 us (1%)
    pallas_call x1, Pallas kernels, shards(): pl.pallas_call(functools.partial(kernel, n_seq, n_head), out_shape=[jax.S...  50.6 us
    pallas_call x1, Pallas kernels, shards(): pl.pallas_call(write_out, out_shape=[jax.ShapeDtypeStruct((tokens, width)...  2.81 us

profile of v3, /device:TPU:0, one launch (start us, length us, event | category | flops | bytes accessed | tf_op | source)
XLA Modules:
  0.0 54.0 jit_solution(10544613716577782250)
XLA Ops:
  0.6 50.6 %lightning.1 = (bf16[512,1024]{1,0:T(8,128)(2,1)}, bf16[512,1024]{1,0:T(8,128)(2,1)}, bf16[512,1024]{1,0:T(8,128)(2,1)}) custom-call(bf16[512,1024]{1,0:T(8,128)(2,1)} %q_hbm.1, bf16[512,1024]{1,0:T(8,128)(2,1)} %k_hbm.1, bf16[512,1024]{1,0:T(8,128)(2,1)} %v_hbm.1, bf16[512,1024]{1,0:T(8,128)(2,1)} %g_hbm.1, f32[8,512]{1,0:T(8,128)} %ld_hbm.1), custom_call_target="tpu_custom_call" | custom-call | tf_op jit(solution)/shard_map/lightning/pallas_call | solution.py:521
  51.2 2.8 %write_out.1 = (bf16[512,1024]{1,0:T(8,128)(2,1)}, bf16[512,1024]{1,0:T(8,128)(2,1)}, bf16[512,1024]{1,0:T(8,128)(2,1)}) custom-call(bf16[512,1024]{1,0:T(8,128)(2,1)} %get-tuple-element.6.q_in, bf16[512,1024]{1,0:T(8,128)(2,1)} %get-tuple-element.7.k_in, bf16[512,1024]{1,0:T(8,128)(2,1)} %get-tuple-element.8.v_in), custom_call_target="tpu_custom_call" | custom-call | tf_op jit(solution)/shard_map/write_out/pallas_call | solution.py:534

commit v4 on v3

--- a/solution.py
+++ b/solution.py
@@ -194,37 +194,46 @@
             device_id={"seq": partner},
         )
 
+    every = range(blocks)
+
     def forward_terms(i):
         h = head_at(i)
         at = columns(i)
-        state = jnp.zeros((DH, DH), f32)
-        for n in range(blocks):
-            to_end = jnp.exp(total_ref[n, pl.ds(h, 1), :] - column_ref[h, rows(n)])
-            end_ref[i, rows(n)] = to_end
-            scaled = (to_end * k_ref[rows(n), at].astype(f32)).astype(bf16)
-            term = dot(scaled, v_ref[rows(n), at], 0, 0)
-            terms[0, i, n] = term
-            state = dec_ref[n, pl.ds(h, 1), :] * state + term
+        to_end = [
+            jnp.exp(total_ref[n, pl.ds(h, 1), :] - column_ref[h, rows(n)]) for n in every
+        ]
+        scaled = [(to_end[n] * k_ref[rows(n), at].astype(f32)).astype(bf16) for n in every]
+        term = [dot(scaled[n], v_ref[rows(n), at], 0, 0) for n in every]
+        state = term[0]
+        for n in every[1:]:
+            state = dec_ref[n, pl.ds(h, 1), :] * state + term[n]
         for c in range(CUTS):
             slab[0, i, c, pl.ds(0, PIECE)] = state[c * PIECE : (c + 1) * PIECE]
             slab[0, i, c, pl.ds(PIECE, 8)] = jnp.broadcast_to(
                 shard_dec_ref[pl.ds(h, 1), :], (8, DH)
             )
+        for n in every:
+            end_ref[i, rows(n)] = to_end[n]
+            terms[0, i, n] = term[n]
 
     def forward_inside(i):
         h = head_at(i)
         at = columns(i)
-        for n in range(blocks):
+        scores = [dot(q_ref[rows(n), at], k_ref[rows(n), at], 1, 1) for n in every]
+        probs = []
+        for n in every:
             row = within_ref[n, pl.ds(h, 1), :]
             column = column_ref[h, rows(n)]
             mask = jnp.where(
                 row_ids >= col_ids, jnp.exp(jnp.minimum(column - row, 0.0)), 0.0
             )
+            probs.append((scores[n] * mask).astype(bf16))
             mask_ref[i, rows(n)] = mask
             grow_ref[i, rows(n)] = jnp.exp(column)
-            probs = (dot(q_ref[rows(n), at], k_ref[rows(n), at], 1, 1) * mask).astype(bf16)
-            probs_ref[i, rows(n)] = probs
-            attn_ref[i, rows(n)] = dot(probs, v_ref[rows(n), at], 1, 0)
+        attn = [dot(probs[n], v_ref[rows(n), at], 1, 0) for n in every]
+        for n in every:
+            probs_ref[i, rows(n)] = probs[n]
+            attn_ref[i, rows(n)] = attn[n]
 
     def loop(low, high, body):
         def step(i, carry):
@@ -290,15 +299,21 @@
         h = head_at(i)
         at = columns(i)
         state = incoming[0, i]
-        for n in range(blocks):
-            rounded = state.astype(bf16)
-            state_ref[i, n] = rounded
-            inter = dot(q_ref[rows(n), at], rounded, 1, 0)
-            attn = attn_ref[i, rows(n)] + grow_ref[i, rows(n)] * inter
-            attn_ref[i, rows(n)] = attn
-            acc_ref[0, rows(n)] += attn * attn
-            acc_ref[1, rows(n)] += attn * g_ref[rows(n), at].astype(f32)
+        rounded = [state.astype(bf16)]
+        for n in every[:-1]:
             state = dec_ref[n, pl.ds(h, 1), :] * state + terms[0, i, n]
+            rounded.append(state.astype(bf16))
+        inter = [dot(q_ref[rows(n), at], rounded[n], 1, 0) for n in every]
+        attn = [attn_ref[i, rows(n)] + grow_ref[i, rows(n)] * inter[n] for n in every]
+        square = [acc_ref[0, rows(n)] + attn[n] * attn[n] for n in every]
+        cross = [
+            acc_ref[1, rows(n)] + attn[n] * g_ref[rows(n), at].astype(f32) for n in every
+        ]
+        for n in every:
+            state_ref[i, n] = rounded[n]
+            attn_ref[i, rows(n)] = attn[n]
+            acc_ref[0, rows(n)] = square[n]
+            acc_ref[1, rows(n)] = cross[n]
 
     def complete_foreign(i):
         for c in range(CUTS):
@@ -362,19 +377,25 @@
     def back_terms(i):
         h = head_at(i)
         at = columns(i)
-        state = jnp.zeros((DH, DH), f32)
-        for n in reversed(range(blocks)):
-            ag = (
+        scaled = [
+            (grow_ref[i, rows(n)] * q_ref[rows(n), at].astype(f32)).astype(bf16) for n in every
+        ]
+        ag = [
+            (
                 row_ref[0, rows(n)]
                 * (g_ref[rows(n), at].astype(f32) - attn_ref[i, rows(n)] * row_ref[1, rows(n)])
             ).astype(bf16)
-            ag_ref[i, rows(n)] = ag
-            scaled = (grow_ref[i, rows(n)] * q_ref[rows(n), at].astype(f32)).astype(bf16)
-            term = dot(scaled, ag, 0, 0)
-            terms[1, i, n] = term
-            state = dec_ref[n, pl.ds(h, 1), :] * state + term
+            for n in every
+        ]
+        term = [dot(scaled[n], ag[n], 0, 0) for n in every]
+        state = term[-1]
+        for n in reversed(every[:-1]):
+            state = dec_ref[n, pl.ds(h, 1), :] * state + term[n]
         for c in range(CUTS):
             slab[1, i, c, pl.ds(0, PIECE)] = state[c * PIECE : (c + 1) * PIECE]
+        for n in every:
+            ag_ref[i, rows(n)] = ag[n]
+            terms[1, i, n] = term[n]
 
     def send_back_terms(i):
         back_terms(i)
@@ -387,14 +408,17 @@
 
     def back_inside(i):
         at = columns(i)
-        for n in range(blocks):
-            ag = ag_ref[i, rows(n)]
-            grad = (dot(ag, v_ref[rows(n), at], 1, 1) * mask_ref[i, rows(n)]).astype(bf16)
-            query = dot(grad, k_ref[rows(n), at], 1, 0)
-            query = query + grow_ref[i, rows(n)] * dot(ag, state_ref[i, n], 1, 1)
-            q_out[i, rows(n)] = query.astype(bf16)
-            ki_ref[i, rows(n)] = dot(grad, q_ref[rows(n), at], 0, 0)
-            vi_ref[i, rows(n)] = dot(probs_ref[i, rows(n)], ag, 0, 0)
+        ag = [ag_ref[i, rows(n)] for n in every]
+        inner = [dot(ag[n], v_ref[rows(n), at], 1, 1) for n in every]
+        inter = [dot(ag[n], state_ref[i, n], 1, 1) for n in every]
+        value = [dot(probs_ref[i, rows(n)], ag[n], 0, 0) for n in every]
+        grad = [(inner[n] * mask_ref[i, rows(n)]).astype(bf16) for n in every]
+        query = [dot(grad[n], k_ref[rows(n), at], 1, 0) for n in every]
+        key = [dot(grad[n], q_ref[rows(n), at], 0, 0) for n in every]
+        for n in every:
+            q_out[i, rows(n)] = (query[n] + grow_ref[i, rows(n)] * inter[n]).astype(bf16)
+            ki_ref[i, rows(n)] = key[n]
+            vi_ref[i, rows(n)] = value[n]
         out_copy(0, i).start()
 
     loop(half, heads, send_back_terms)
@@ -404,14 +428,16 @@
         h = head_at(i)
         at = columns(i)
         state = incoming[1, i]
-        for n in reversed(range(blocks)):
-            rounded = state.astype(bf16)
+        rounded = [state.astype(bf16)]
+        for n in reversed(every[1:]):
+            state = dec_ref[n, pl.ds(h, 1), :] * state + terms[1, i, n]
+            rounded.insert(0, state.astype(bf16))
+        key = [dot(v_ref[rows(n), at], rounded[n], 1, 1) for n in every]
+        value = [dot(k_ref[rows(n), at], rounded[n], 1, 0) for n in every]
+        for n in every:
             to_end = end_ref[i, rows(n)]
-            key = ki_ref[i, rows(n)] + to_end * dot(v_ref[rows(n), at], rounded, 1, 1)
-            value = vi_ref[i, rows(n)] + to_end * dot(k_ref[rows(n), at], rounded, 1, 0)
-            k_out[i, rows(n)] = key.astype(bf16)
-            v_out[i, rows(n)] = value.astype(bf16)
-            state = dec_ref[n, pl.ds(h, 1), :] * state + terms[1, i, n]
+            k_out[i, rows(n)] = (ki_ref[i, rows(n)] + to_end * key[n]).astype(bf16)
+            v_out[i, rows(n)] = (vi_ref[i, rows(n)] + to_end * value[n]).astype(bf16)
         out_copy(1, i).start()
         out_copy(2, i).start()
 

time: 54.3 us -> 53.8 us (level)
  no operation moved by 1% of the time
where the time goes in v4:
time: 53.8 us; the launch traced here: 53.5 us
  Pallas kernels  52.9 us (98%)
  between operations  0.64 us (1%)
    pallas_call x1, Pallas kernels, shards(): pl.pallas_call(functools.partial(kernel, n_seq, n_head), out_shape=[jax.S...  50.1 us
    pallas_call x1, Pallas kernels, shards(): pl.pallas_call(write_out, out_shape=[jax.ShapeDtypeStruct((tokens, width)...  2.81 us

profile of v4, /device:TPU:0, one launch (start us, length us, event | category | flops | bytes accessed | tf_op | source)
XLA Modules:
  0.0 53.5 jit_solution(1369888016443288341)
XLA Ops:
  0.6 50.1 %lightning.1 = (bf16[512,1024]{1,0:T(8,128)(2,1)}, bf16[512,1024]{1,0:T(8,128)(2,1)}, bf16[512,1024]{1,0:T(8,128)(2,1)}) custom-call(bf16[512,1024]{1,0:T(8,128)(2,1)} %q_hbm.1, bf16[512,1024]{1,0:T(8,128)(2,1)} %k_hbm.1, bf16[512,1024]{1,0:T(8,128)(2,1)} %v_hbm.1, bf16[512,1024]{1,0:T(8,128)(2,1)} %g_hbm.1, f32[8,512]{1,0:T(8,128)} %ld_hbm.1), custom_call_target="tpu_custom_call" | custom-call | tf_op jit(solution)/shard_map/lightning/pallas_call | solution.py:547
  50.7 2.8 %write_out.1 = (bf16[512,1024]{1,0:T(8,128)(2,1)}, bf16[512,1024]{1,0:T(8,128)(2,1)}, bf16[512,1024]{1,0:T(8,128)(2,1)}) custom-call(bf16[512,1024]{1,0:T(8,128)(2,1)} %get-tuple-element.6.q_in, bf16[512,1024]{1,0:T(8,128)(2,1)} %get-tuple-element.7.k_in, bf16[512,1024]{1,0:T(8,128)(2,1)} %get-tuple-element.8.v_in), custom_call_target="tpu_custom_call" | custom-call | tf_op jit(solution)/shard_map/write_out/pallas_call | solution.py:560

commit v5 on v4

--- a/solution.py
+++ b/solution.py
@@ -136,27 +136,24 @@
     row_ids = lax.broadcasted_iota(jnp.int32, (BLOCK, BLOCK), 0)
     col_ids = lax.broadcasted_iota(jnp.int32, (BLOCK, BLOCK), 1)
     loads[0].wait()
-    upto = (row_ids <= col_ids).astype(f32)
-    since = (row_ids >= col_ids).astype(f32)
+    upto = (row_ids <= col_ids).astype(bf16)
+    since = (row_ids >= col_ids).astype(bf16)
+    rest = jnp.concatenate([ld_ref[:, rows(n)] for n in range(blocks)], axis=0)
+    parts = []
+    for _ in range(3):
+        parts.append(rest.astype(bf16))
+        rest = rest - parts[-1].astype(f32)
+    all_within = sum(dot(part, upto, 1, 0) for part in parts[::-1])
+    by_column = sum(dot(since, part, 1, 1) for part in parts[::-1])
     shard_total = jnp.zeros((heads, BLOCK), f32)
     for n in range(blocks):
-        within = lax.dot_general(
-            ld_ref[:, rows(n)],
-            upto,
-            (((1,), (0,)), ((), ())),
-            precision=lax.Precision.HIGHEST,
-            preferred_element_type=f32,
-        )
+        within = all_within[n * heads : (n + 1) * heads]
         total = jnp.broadcast_to(within[:, BLOCK - 1 : BLOCK], (heads, BLOCK))
-        by_column = lax.dot_general(
-            since,
-            ld_ref[:, rows(n)],
-            (((1,), (1,)), ((), ())),
-            precision=lax.Precision.HIGHEST,
-            preferred_element_type=f32,
-        )
         for h in range(heads):
-            column_ref[h, rows(n)] = jnp.broadcast_to(by_column[:, h : h + 1], (BLOCK, BLOCK))
+            lane = n * heads + h
+            column_ref[h, rows(n)] = jnp.broadcast_to(
+                by_column[:, lane : lane + 1], (BLOCK, BLOCK)
+            )
         within_ref[n] = within
         total_ref[n] = total
         dec_ref[n] = jnp.exp(total)
@@ -333,7 +330,7 @@
         return unit
 
     def run(d, at, inside, after, after_foreign):
-        ahead = (at * heads) // max(groups - 1, 1)
+        ahead = jnp.minimum(at, heads)
         loop(0, ahead, inside)
         scan(d, units(ahead, inside, after))
         loop(ahead + half, heads, inside)

time: 53.8 us -> 54.2 us (level)
  no operation moved by 1% of the time
where the time goes in v5:
time: 54.2 us; the launch traced here: 54 us
  Pallas kernels  53.3 us (98%)
  between operations  0.64 us (1%)
    pallas_call x1, Pallas kernels, shards(): pl.pallas_call(functools.partial(kernel, n_seq, n_head), out_shape=[jax.S...  50.5 us
    pallas_call x1, Pallas kernels, shards(): pl.pallas_call(write_out, out_shape=[jax.ShapeDtypeStruct((tokens, width)...  2.81 us

profile of v5, /device:TPU:0, one launch (start us, length us, event | category | flops | bytes accessed | tf_op | source)
XLA Modules:
  0.0 54.0 jit_solution(6268665093996994784)
XLA Ops:
  0.6 50.5 %lightning.1 = (bf16[512,1024]{1,0:T(8,128)(2,1)}, bf16[512,1024]{1,0:T(8,128)(2,1)}, bf16[512,1024]{1,0:T(8,128)(2,1)}) custom-call(bf16[512,1024]{1,0:T(8,128)(2,1)} %q_hbm.1, bf16[512,1024]{1,0:T(8,128)(2,1)} %k_hbm.1, bf16[512,1024]{1,0:T(8,128)(2,1)} %v_hbm.1, bf16[512,1024]{1,0:T(8,128)(2,1)} %g_hbm.1, f32[8,512]{1,0:T(8,128)} %ld_hbm.1), custom_call_target="tpu_custom_call" | custom-call | tf_op jit(solution)/shard_map/lightning/pallas_call | solution.py:544
  51.2 2.8 %write_out.1 = (bf16[512,1024]{1,0:T(8,128)(2,1)}, bf16[512,1024]{1,0:T(8,128)(2,1)}, bf16[512,1024]{1,0:T(8,128)(2,1)}) custom-call(bf16[512,1024]{1,0:T(8,128)(2,1)} %get-tuple-element.6.q_in, bf16[512,1024]{1,0:T(8,128)(2,1)} %get-tuple-element.7.k_in, bf16[512,1024]{1,0:T(8,128)(2,1)} %get-tuple-element.8.v_in), custom_call_target="tpu_custom_call" | custom-call | tf_op jit(solution)/shard_map/write_out/pallas_call | solution.py:557

commit v6 on v5

--- a/solution.py
+++ b/solution.py
@@ -159,14 +159,11 @@
         dec_ref[n] = jnp.exp(total)
         shard_total = shard_total + total
     shard_dec_ref[...] = jnp.exp(shard_total)
-    loads[1].wait()
-    loads[2].wait()
-
-    def pair_copy(d, i, c):
+
+    def pair_copy(d, j, c):
         size = PIECE + 8 if d == 0 else PIECE
-        j = i - half
         return pltpu.make_async_remote_copy(
-            src_ref=slab.at[d, i, c, pl.ds(0, size)],
+            src_ref=slab.at[d, half + j, c, pl.ds(0, size)],
             dst_ref=pair_in.at[d, j, c, pl.ds(0, size)],
             send_sem=pair_send.at[d, j, c],
             recv_sem=pair_recv.at[d, j, c],
@@ -245,7 +242,7 @@
 
         def step(j):
             for c in range(CUTS):
-                pair_copy(d, half + j, c).wait_recv()
+                pair_copy(d, j, c).wait_recv()
 
                 @pl.when(at > 0)
                 def _():
@@ -268,11 +265,11 @@
 
                 @pl.when(at < groups - 1)
                 def _():
-                    chain_copy(d, j, c).start()
+                    in_turn(chain_copy, d, j, c)
 
                 incoming[d, j, pl.ds(c * PIECE, PIECE)] = jnp.where(first, before, between)
                 pair_out[d, j, c] = jnp.where(first, between, before)
-                fin_copy(d, j, c).start()
+                in_turn(fin_copy, d, j, c)
             unit(j)
 
         loop(0, half, step)
@@ -280,15 +277,25 @@
     n_peers = 1 + (z > 0).astype(jnp.int32) + (z < groups - 1).astype(jnp.int32) + n_head - 1
     pl.semaphore_wait(barrier, n_peers)
 
-    def send_terms(i):
-        forward_terms(i)
-        for c in range(CUTS):
-            pair_copy(0, i, c).start()
-
-    loop(half, heads, send_terms)
-    loads[3].wait()
-    loads[4].wait()
-    loop(0, half, forward_terms)
+    def in_turn(copy, d, j, c):
+        @pl.when(j > 0)
+        def _():
+            copy(d, j - 1, c).wait_send()
+
+        copy(d, j, c).start()
+
+    def exchange(d, body):
+        def step(j):
+            body(half + j)
+            for c in range(CUTS):
+                in_turn(pair_copy, d, j, c)
+            body(j)
+
+        loop(0, half, step)
+
+    for load in loads[1:5]:
+        load.wait()
+    exchange(0, forward_terms)
     loads[5].wait()
     acc_ref[...] = jnp.zeros_like(acc_ref)
 
@@ -394,11 +401,6 @@
             ag_ref[i, rows(n)] = ag[n]
             terms[1, i, n] = term[n]
 
-    def send_back_terms(i):
-        back_terms(i)
-        for c in range(CUTS):
-            pair_copy(1, i, c).start()
-
     def out_copy(which, i):
         src, dst = ((q_out, qo_hbm), (k_out, ko_hbm), (v_out, vo_hbm))[which]
         return pltpu.make_async_copy(src.at[i], dst.at[:, columns(i)], out_sem.at[which, i])
@@ -418,8 +420,7 @@
             vi_ref[i, rows(n)] = value[n]
         out_copy(0, i).start()
 
-    loop(half, heads, send_back_terms)
-    loop(0, half, back_terms)
+    exchange(1, back_terms)
 
     def finish(i):
         h = head_at(i)
@@ -449,16 +450,13 @@
         stat_copy(step).wait_send()
     for d in range(2):
 
-        def drain(j):
-            for c in range(CUTS):
-                pair_copy(d, half + j, c).wait_send()
-                fin_copy(d, j, c).wait_send()
-
-                @pl.when((z < groups - 1) if d == 0 else (z > 0))
-                def _():
-                    chain_copy(d, j, c).wait_send()
-
-        loop(0, half, drain)
+        for c in range(CUTS):
+            pair_copy(d, half - 1, c).wait_send()
+            fin_copy(d, half - 1, c).wait_send()
+
+            @pl.when((z < groups - 1) if d == 0 else (z > 0))
+            def _():
+                chain_copy(d, half - 1, c).wait_send()
 
     def drain_out(i):
         for which in range(3):

time: 54.2 us -> 62.6 us (1.15)
  Pallas kernels: 53.3 us -> 61.7 us
    pallas_call x1, Pallas kernels: 50.5 us -> 58.9 us  [shards(): pl.pallas_call(functools.partial(kernel, n_seq, n_head), out_shape=[jax.S...]
where the time goes in v6:
time: 62.6 us; the launch traced here: 62.3 us
  Pallas kernels  61.7 us (99%)
  between operations  0.64 us (1%)
    pallas_call x1, Pallas kernels, shards(): pl.pallas_call(functools.partial(kernel, n_seq, n_head), out_shape=[jax.S...  58.9 us
    pallas_call x1, Pallas kernels, shards(): pl.pallas_call(write_out, out_shape=[jax.ShapeDtypeStruct((tokens, width)...  2.81 us

profile of v6, /device:TPU:0, one launch (start us, length us, event | category | flops | bytes accessed | tf_op | source)
XLA Modules:
  0.0 62.3 jit_solution(11949126886573582832)
XLA Ops:
  0.6 58.9 %lightning.1 = (bf16[512,1024]{1,0:T(8,128)(2,1)}, bf16[512,1024]{1,0:T(8,128)(2,1)}, bf16[512,1024]{1,0:T(8,128)(2,1)}) custom-call(bf16[512,1024]{1,0:T(8,128)(2,1)} %q_hbm.1, bf16[512,1024]{1,0:T(8,128)(2,1)} %k_hbm.1, bf16[512,1024]{1,0:T(8,128)(2,1)} %v_hbm.1, bf16[512,1024]{1,0:T(8,128)(2,1)} %g_hbm.1, f32[8,512]{1,0:T(8,128)} %ld_hbm.1), custom_call_target="tpu_custom_call" | custom-call | tf_op jit(solution)/shard_map/lightning/pallas_call | solution.py:542
  59.5 2.8 %write_out.1 = (bf16[512,1024]{1,0:T(8,128)(2,1)}, bf16[512,1024]{1,0:T(8,128)(2,1)}, bf16[512,1024]{1,0:T(8,128)(2,1)}) custom-call(bf16[512,1024]{1,0:T(8,128)(2,1)} %get-tuple-element.6.q_in, bf16[512,1024]{1,0:T(8,128)(2,1)} %get-tuple-element.7.k_in, bf16[512,1024]{1,0:T(8,128)(2,1)} %get-tuple-element.8.v_in), custom_call_target="tpu_custom_call" | custom-call | tf_op jit(solution)/shard_map/write_out/pallas_call | solution.py:555

commit v7 on v5

--- a/solution.py
+++ b/solution.py
@@ -10,7 +10,7 @@
 HEAD_COUNT = 32
 DH = 128
 BLOCK = 128
-CUTS = 2
+CUTS = 4
 PIECE = DH // CUTS
 VMEM_LIMIT = 61 * 1024 * 1024
 EPSILON = 1e-06

time: 54.2 us -> 54.5 us (level)
  no operation moved by 1% of the time
where the time goes in v7:
time: 54.5 us; the launch traced here: 54.3 us
  Pallas kernels  53.6 us (98%)
  between operations  0.64 us (1%)
    pallas_call x1, Pallas kernels, shards(): pl.pallas_call(functools.partial(kernel, n_seq, n_head), out_shape=[jax.S...  50.8 us
    pallas_call x1, Pallas kernels, shards(): pl.pallas_call(write_out, out_shape=[jax.ShapeDtypeStruct((tokens, width)...  2.81 us

profile of v7, /device:TPU:0, one launch (start us, length us, event | category | flops | bytes accessed | tf_op | source)
XLA Modules:
  0.0 54.3 jit_solution(1460490589564371920)
XLA Ops:
  0.6 50.8 %lightning.1 = (bf16[512,1024]{1,0:T(8,128)(2,1)}, bf16[512,1024]{1,0:T(8,128)(2,1)}, bf16[512,1024]{1,0:T(8,128)(2,1)}) custom-call(bf16[512,1024]{1,0:T(8,128)(2,1)} %q_hbm.1, bf16[512,1024]{1,0:T(8,128)(2,1)} %k_hbm.1, bf16[512,1024]{1,0:T(8,128)(2,1)} %v_hbm.1, bf16[512,1024]{1,0:T(8,128)(2,1)} %g_hbm.1, f32[8,512]{1,0:T(8,128)} %ld_hbm.1), custom_call_target="tpu_custom_call" | custom-call | tf_op jit(solution)/shard_map/lightning/pallas_call | solution.py:544
  51.5 2.8 %write_out.1 = (bf16[512,1024]{1,0:T(8,128)(2,1)}, bf16[512,1024]{1,0:T(8,128)(2,1)}, bf16[512,1024]{1,0:T(8,128)(2,1)}) custom-call(bf16[512,1024]{1,0:T(8,128)(2,1)} %get-tuple-element.6.q_in, bf16[512,1024]{1,0:T(8,128)(2,1)} %get-tuple-element.7.k_in, bf16[512,1024]{1,0:T(8,128)(2,1)} %get-tuple-element.8.v_in), custom_call_target="tpu_custom_call" | custom-call | tf_op jit(solution)/shard_map/write_out/pallas_call | solution.py:557
